TPU v7x, 512 devices: a whole 4x8x8 slice. The times are simulated.
512 devices in a mesh: ctx: 64 (over x, z, core), tp: 8 (over y).
Axes of the slice: x: 4, y: 8, z: 8, core: 2. Of those that a mesh axis runs over, the one named last changes fastest.
Arguments:
- kv_cache: bfloat16 [262144, 2048], P('ctx', 'tp'), may hold values from -6 to 6
- page_session: int32 [4096], P('ctx'), may hold values from 0 to 3
- queries: bfloat16 [256, 8192], P(None, 'tp'), may hold values from -12 to 12
- tree_kv: bfloat16 [256, 2048], P(None, 'tp'), may hold values from -12 to 12
- tree_parent: int32 [4, 64], replicated, may hold values from -1 to 62, as said below
- move_count: int32 [64, 64], replicated, may hold values from 0 to 1, as said below
- draft_states: bfloat16 [256, 4096], P(None, 'ctx'), may hold values from -20 to 20
- accept_node: int32 [4, 8], replicated, may hold values from 0 to 63
- w_gate: bfloat16 [4096, 14336], P('ctx', 'tp'), may hold values from -0.09375 to 0.09375
- w_up: bfloat16 [4096, 14336], P('ctx', 'tp'), may hold values from -0.09375 to 0.09375
- w_down: bfloat16 [14336, 4096], P('tp', 'ctx'), may hold values from -0.046875 to 0.046875
Outputs:
- attn_out: bfloat16 [256, 8192], P('ctx', 'tp')
- arrived: bfloat16 [131072, 2048], P('ctx', 'tp')
- draft_out: bfloat16 [32, 4096], P(None, 'ctx')
Inputs may be any that keep to these rules, and one draw needn't show every extreme that they name: Each tree_parent[s, i] is -1 or a node below i. `move_count`: each shard sends to at most 32 shards and receives from at most 32; every row and every column sums to at most 32, and some row and some column reach it.
All inputs are finite; a program needn't handle non-finite values.
Results may differ from a plain program's by a relative error of at most 0.005.
Values may be sent and summed in bfloat16 or wider, within the bound.
A program may use at most 128 MiB of HBM per device.

v0:
```python
import math

import jax
import jax.numpy as jnp
from jax import lax
from jax.sharding import PartitionSpec as P

HD = 128
QH = 64
KVH = 8
DD = 4096
PAGE = 64
SESS = 4
MOVE_PAIR = 1
NODES = 64
ROWS = 256


def ancestors(parents):
    count = parents.shape[0]
    nodes = jnp.arange(count, dtype=jnp.int32)
    link = (parents[:, None] == nodes[None, :]).astype(jnp.float32)
    reach = link + jnp.eye(count, dtype=jnp.float32)
    for repeat in range(count.bit_length()):
        reach = jnp.minimum(jnp.dot(reach, reach, precision=lax.Precision.HIGHEST), 1.0)
    return reach


def migrate(kv_cache, move_count):
    myself = lax.axis_index("ctx")
    peers = move_count.shape[0]
    capacity = peers // 2 * MOVE_PAIR
    width = kv_cache.shape[1]
    pages = kv_cache.reshape(-1, PAGE, width)
    page_total = pages.shape[0]
    outgoing_row = move_count[myself]
    send_start = jnp.cumsum(outgoing_row) - outgoing_row
    slot = jnp.arange(MOVE_PAIR, dtype=jnp.int32)
    local = jnp.clip(send_start[:, None] + slot[None, :], 0, page_total - 1)
    live = slot[None, :] < outgoing_row[:, None]
    picked = pages[local]
    outgoing = jnp.where(live[:, :, None, None], picked, jnp.zeros_like(picked))
    incoming = lax.all_to_all(outgoing, "ctx", split_axis=0, concat_axis=0, tiled=True)
    incoming_col = move_count[:, myself]
    ends = jnp.cumsum(incoming_col)
    starts = ends - incoming_col
    slots = jnp.arange(capacity, dtype=jnp.int32)
    source = jnp.sum((ends[None, :] <= slots[:, None]).astype(jnp.int32), axis=1)
    valid = slots < ends[peers - 1]
    source = jnp.minimum(source, peers - 1)
    flat = jnp.clip(source * MOVE_PAIR + slots - starts[source], 0, peers * MOVE_PAIR - 1)
    placed = incoming.reshape(peers * MOVE_PAIR, PAGE, width)[flat]
    placed = jnp.where(valid[:, None, None], placed, jnp.zeros_like(placed))
    return placed.reshape(capacity * PAGE, width)


def body(
    kv_cache,
    page_session,
    queries,
    tree_kv,
    tree_parent,
    move_count,
    draft_states,
    accept_node,
    w_gate,
    w_up,
    w_down,
):
    arrived = migrate(kv_cache, move_count)
    group = QH // KVH
    scale = 1.0 / math.sqrt(HD)
    reach = jax.vmap(ancestors)(tree_parent) > 0.5
    token_session = jnp.repeat(page_session, PAGE)
    cache_scores = []
    tree_scores = []
    cache_top = []
    tree_top = []
    head_local = 0
    base = head_local * 2 * HD
    keys = kv_cache[:, base : base + HD]
    tree_keys = tree_kv[:, base : base + HD]
    for session in range(SESS):
        rows = queries[
            session * NODES : (session + 1) * NODES,
            head_local * group * HD : (head_local + 1) * group * HD,
        ].reshape(NODES * group, HD)
        scores = jnp.einsum("qd,kd->qk", rows, keys, preferred_element_type=jnp.float32) * scale
        scores = jnp.where(token_session[None, :] == session, scores, -jnp.inf)
        own_keys = tree_keys[session * NODES : (session + 1) * NODES]
        branch = jnp.einsum("qd,kd->qk", rows, own_keys, preferred_element_type=jnp.float32) * scale
        branch = jnp.where(jnp.repeat(reach[session], group, axis=0), branch, -jnp.inf)
        cache_scores.append(scores)
        tree_scores.append(branch)
        cache_top.append(jnp.max(scores, axis=1).reshape(NODES, group))
        tree_top.append(jnp.max(branch, axis=1).reshape(NODES, group))

    def assemble(blocks):
        columns = jnp.concatenate(blocks[0:SESS], axis=0)
        return columns

    global_cache_top = lax.pmax(assemble(cache_top), "ctx")
    top = jnp.maximum(global_cache_top, assemble(tree_top))
    cache_acc = []
    cache_tot = []
    tree_acc = []
    tree_tot = []
    head_local = 0
    base = head_local * 2 * HD
    values = kv_cache[:, base + HD : base + 2 * HD]
    tree_values = tree_kv[:, base + HD : base + 2 * HD]
    for session in range(SESS):
        index = head_local * SESS + session
        row_top = top[
            session * NODES : (session + 1) * NODES, head_local * group : (head_local + 1) * group
        ].reshape(NODES * group)
        weights = jnp.exp(cache_scores[index] - row_top[:, None])
        tree_weights = jnp.exp(tree_scores[index] - row_top[:, None])
        own_values = tree_values[session * NODES : (session + 1) * NODES]
        cache_tot.append(jnp.sum(weights, axis=1).reshape(NODES, group))
        tree_tot.append(jnp.sum(tree_weights, axis=1).reshape(NODES, group))
        cache_acc.append(
            jnp.dot(
                weights.astype(jnp.bfloat16), values, preferred_element_type=jnp.float32
            ).reshape(NODES, group * HD)
        )
        tree_acc.append(
            jnp.dot(
                tree_weights.astype(jnp.bfloat16), own_values, preferred_element_type=jnp.float32
            ).reshape(NODES, group * HD)
        )
    cache_sums = assemble(cache_acc)
    cache_totals = assemble(cache_tot)
    tree_sums = assemble(tree_acc)
    tree_totals = assemble(tree_tot)
    rows_dev = ROWS // lax.axis_size("ctx")
    start = lax.axis_index("ctx") * rows_dev
    summed, totals = lax.psum((cache_sums, cache_totals), "ctx")
    summed = lax.dynamic_slice_in_dim(summed, start, rows_dev, 0)
    totals = lax.dynamic_slice_in_dim(totals, start, rows_dev, 0)
    summed = summed + lax.dynamic_slice_in_dim(tree_sums, start, rows_dev, 0)
    totals = totals + lax.dynamic_slice_in_dim(tree_totals, start, rows_dev, 0)
    heads_dev = totals.shape[1]
    attn_out = (
        (summed.reshape(rows_dev, heads_dev, HD) / totals[:, :, None])
        .reshape(rows_dev, heads_dev * HD)
        .astype(jnp.bfloat16)
    )
    rows_index = (jnp.arange(SESS, dtype=jnp.int32)[:, None] * NODES + accept_node).reshape(-1)
    chosen = draft_states[rows_index]
    widened = chosen.astype(jnp.float32)
    squares = jnp.sum(widened * widened, axis=1)
    partial_gate = jnp.dot(chosen, w_gate, preferred_element_type=jnp.float32)
    partial_up = jnp.dot(chosen, w_up, preferred_element_type=jnp.float32)
    gate, up_proj, square_sum = lax.psum((partial_gate, partial_up, squares), "ctx")
    inverse = lax.rsqrt(square_sum / DD + 1e-05)
    hidden = (jax.nn.silu(inverse[:, None] * gate) * (inverse[:, None] * up_proj)).astype(
        jnp.bfloat16
    )
    draft_terms = jnp.dot(hidden, w_down, preferred_element_type=jnp.float32)
    draft_out = lax.psum(draft_terms, "tp").astype(jnp.bfloat16)
    return (attn_out, arrived, draft_out)


def solution(mesh):
    placed = (
        P("ctx", "tp"),
        P("ctx"),
        P(None, "tp"),
        P(None, "tp"),
        P(),
        P(),
        P(None, "ctx"),
        P(),
        P("ctx", "tp"),
        P("ctx", "tp"),
        P("tp", "ctx"),
    )
    return jax.shard_map(
        body,
        mesh=mesh,
        in_specs=placed,
        out_specs=(P("ctx", "tp"), P("ctx", "tp"), P(None, "ctx")),
        check_vma=False,
    )
```

profile of v0, /device:TPU:1, one launch (start us, length us, event | category | flops | bytes accessed | tf_op | source)
XLA Modules:
  0.0 463.4 jit_solution(9811693064247077610)
XLA Ops:
  7.2 0.8 fusion.88
  8.8 1.2 fusion.105
  10.0 3.8 gather_fusion
  13.8 3.2 bitcast_select_fusion
  17.0 15.0 %all-to-all-start = ((bf16[64,1,64,256]{3,2,1,0:T(8,128)(2,1)}), bf16[64,1,64,256]{3,2,1,0:T(8,128)(2,1)}, u32[]{:S(2)}, u32[]{:S(2)}) async-start(bf16[64,1,64,256]{3,2,1,0:T(8,128)(2,1)} %bitcast_select_fusion), calls=%async_computation | async-start | bytes 4194304 | tf_op jit(solution)/shard_map/all_to_all | solution.py:43
  34.9 4.6 fusion.3
  39.8 4.6 fusion.2
  44.8 4.6 fusion.1
  49.7 4.6 fusion
  54.5 143.8 %pmax.7 = f32[256,8]{0,1:T(8,128)S(1)} all-reduce(f32[256,8]{0,1:T(8,128)S(1)} %pad_maximum_fusion.1), channel_id=1, replica_groups=mesh['ctx'=64,'tp'=8] {'ctx'}, use_global_device_ids=true, to_apply=%region_4.5 | all-reduce | flops 2048 | bytes 16384 | tf_op jit(solution)/shard_map/pmax | solution.py:102
  201.7 5.1 %fusion.12 = f32[512,128]{1,0:T(8,128)S(1)} fusion(f32[512,4096]{1,0:T(8,128)} %get-tuple-element.27, f32[512]{0:T(512)S(1)} %sub.105, pred[4096]{0:T(1024)(128)(4,1)S(1)} %eq.91, bf16[4096,256]{1,0:T(8,128)(2,1)S(1)} %copy-done.1), kind=kOutput, calls=%fused_computation.24 | convolution fusion | flops 545259520 | bytes 9705472 | tf_op jit(solution)/shard_map/dot_general | solution.py:123
  206.8 5.8 %fusion.14 = f32[512,128]{1,0:T(8,128)} fusion(f32[512,4096]{1,0:T(8,128)} %get-tuple-element.29, f32[512]{0:T(512)S(1)} %sub.102, pred[4096]{0:T(1024)(128)(4,1)S(1)} %eq.88, bf16[4096,256]{1,0:T(8,128)(2,1)S(1)} %copy-done.1), kind=kOutput, calls=%fused_computation.25 | convolution fusion | flops 545259520 | bytes 9705472 | tf_op jit(solution)/shard_map/dot_general | solution.py:123
  212.6 1.0 reshape.336
  213.6 5.8 %fusion.16 = f32[512,128]{1,0:T(8,128)} fusion(f32[512,4096]{1,0:T(8,128)} %get-tuple-element.31, f32[512]{0:T(512)S(1)} %sub.99, pred[4096]{0:T(1024)(128)(4,1)S(1)} %eq.85, bf16[4096,256]{1,0:T(8,128)(2,1)S(1)} %copy-done.1), kind=kOutput, calls=%fused_computation.26 | convolution fusion | flops 545259520 | bytes 9705472 | tf_op jit(solution)/shard_map/dot_general | solution.py:123
  219.4 1.7 reshape.335
  221.1 5.8 %fusion.18 = f32[512,128]{1,0:T(8,128)} fusion(f32[512,4096]{1,0:T(8,128)} %get-tuple-element.33, f32[512]{0:T(512)S(1)} %sub.96, pred[4096]{0:T(1024)(128)(4,1)S(1)} %eq.82, bf16[4096,256]{1,0:T(8,128)(2,1)S(1)} %copy-done.1), kind=kOutput, calls=%fused_computation.27 | convolution fusion | flops 545259520 | bytes 9705472 | tf_op jit(solution)/shard_map/dot_general | solution.py:123
  226.9 1.0 reshape.334
  228.5 0.9 fusion.107
  229.4 1.8 fusion.106
  231.2 2.0 pad_maximum_fusion
  233.2 4.7 %fusion.10 = f32[512]{0:T(512)S(1)} fusion(f32[512,4096]{1,0:T(8,128)} %get-tuple-element.27, f32[512]{0:T(512)S(1)} %sub.105, pred[4096]{0:T(1024)(128)(4,1)S(1)} %eq.91), kind=kLoop, calls=%fused_computation.22 | loop fusion | flops 8388096 | bytes 8396800 | tf_op jit(solution)/shard_map/reduce_sum | solution.py:120
  237.9 4.5 fusion.8
  244.1 4.6 fusion.6
  248.9 4.6 fusion.4
  253.8 129.1 %all-reduce = (f32[256,8]{0,1:T(8,128)S(1)}, f32[32]{0:T(128)S(1)}) all-reduce(f32[256,8]{0,1:T(8,128)S(1)} %pad_maximum_fusion.2, f32[32]{0:T(128)S(1)} %multiply_reduce_fusion), channel_id=1, replica_groups=mesh['ctx'=64,'tp'=8] {'ctx'}, use_global_device_ids=true, to_apply=%region_14.15 | all-reduce | flops 2080 | bytes 16640 | tf_op jit(solution)/shard_map/psum | solution.py:138
  385.1 0.7 gather_fusion.1
  385.9 41.0 %all-reduce.4.cloned.1.call-done = (f32[256,1024]{1,0:T(8,128)}, f32[32,1792]{1,0:T(8,128)}, f32[32,1792]{1,0:T(8,128)}) async-done(((f32[256,1024]{1,0:T(8,128)}, f32[32,1792]{1,0:T(8,128)}, f32[32,1792]{1,0:T(8,128)}), (f32[256,1024]{1,0:T(8,128)}, f32[32,1792]{1,0:T(8,128)}, f32[32,1792]{1,0:T(8,128)})) %all-reduce.4.cloned.1.call-update) | async-done | bytes 1507344 | tf_op jit(solution)/shard_map/psum | solution.py:138
  426.9 1.3 fusion.52
  428.2 23.4 %psum.47 = bf16[32,64]{1,0:T(8,128)(2,1)} all-reduce(f32[32,64]{1,0:T(8,128)S(1)} %fusion.52), channel_id=1, replica_groups=mesh['ctx'=64,'tp'=8] {'tp'}, use_global_device_ids=true, to_apply=%region_26.27 | all-reduce | flops 2048 | bytes 12288 | tf_op jit(solution)/shard_map/psum | solution.py:161
  451.6 1.4 fusion.79
  453.0 2.2 gather_fusion.2
  455.2 1.3 bitcast_select_fusion.1
  (142 shorter events, 13.1 us)
Async XLA Ops:
  7.2 221.3 %copy-start = (bf16[64,1792]{1,0:T(8,128)(2,1)S(1)}, bf16[64,1792]{1,0:T(8,128)(2,1)}, u32[]{:S(2)}) copy-start(bf16[64,1792]{1,0:T(8,128)(2,1)} %param.20) | copy-start | bytes 688132
  7.2 24.9 %copy-start.6 = (s32[64,64]{1,0:T(8,128)S(1)}, s32[64,64]{1,0:T(8,128)}, u32[]{:S(2)}) copy-start(s32[64,64]{1,0:T(8,128)} %param.16) | copy-start | bytes 49156
  7.2 25.1 %copy-start.8 = (s32[4,64]{1,0:T(4,128)S(1)}, s32[4,64]{1,0:T(4,128)}, u32[]{:S(2)}) copy-start(s32[4,64]{1,0:T(4,128)} %param.15) | copy-start | bytes 3076
  7.2 27.3 %copy-start.2 = (bf16[256,1024]{1,0:T(8,128)(2,1)S(1)}, bf16[256,1024]{1,0:T(8,128)(2,1)}, u32[]{:S(2)}) copy-start(bf16[256,1024]{1,0:T(8,128)(2,1)} %param.13) | copy-start | bytes 1572868
  10.0 24.6 %copy-start.9 = (s32[64]{0:T(128)S(1)}, s32[64]{0:T(128)}, u32[]{:S(2)}) copy-start(s32[64]{0:T(128)} %param.12) | copy-start | bytes 772
  10.0 24.8 %copy-start.1 = (bf16[4096,256]{1,0:T(8,128)(2,1)S(1)}, bf16[4096,256]{1,0:T(8,128)(2,1)}, u32[]{:S(2)}) copy-start(bf16[4096,256]{1,0:T(8,128)(2,1)} %param.11) | copy-start | bytes 6291460
  17.0 436.0 %all-to-all-start = ((bf16[64,1,64,256]{3,2,1,0:T(8,128)(2,1)}), bf16[64,1,64,256]{3,2,1,0:T(8,128)(2,1)}, u32[]{:S(2)}, u32[]{:S(2)}) async-start(bf16[64,1,64,256]{3,2,1,0:T(8,128)(2,1)} %bitcast_select_fusion), calls=%async_computation | async-start | bytes 4194304 | tf_op jit(solution)/shard_map/all_to_all | solution.py:43
  32.0 394.9 %all-reduce.4.cloned.1.call-start = ((), (), s32[]{:S(2)}) async-start(), calls=%async_computation.1 | async-start | bytes 3014656 | tf_op jit(solution)/shard_map/psum | solution.py:138
  49.4 149.1 %copy-start.3 = (bf16[256,256]{1,0:T(8,128)(2,1)S(1)}, bf16[256,256]{1,0:T(8,128)(2,1)}, u32[]{:S(2)}) copy-start(bf16[256,256]{1,0:T(8,128)(2,1)} %param.14) | copy-start | bytes 393220
  49.4 151.7 %copy-start.5 = (bf16[256,64]{0,1:T(8,128)(2,1)S(1)}, bf16[256,64]{0,1:T(8,128)(2,1)}, u32[]{:S(2)}) copy-start(bf16[256,64]{0,1:T(8,128)(2,1)} %param.17) | copy-start | bytes 98308
  49.4 152.1 %copy-start.7 = (s32[4,8]{1,0:T(4,128)S(1)}, s32[4,8]{1,0:T(4,128)}, u32[]{:S(2)}) copy-start(s32[4,8]{1,0:T(4,128)} %param.18) | copy-start | bytes 388
  244.1 139.0 %copy-start.4 = (bf16[256,256]{1,0:T(8,128)(2,1)S(1)}, bf16[256,256]{1,0:T(8,128)(2,1)}, u32[]{:S(2)}) copy-start(bf16[256,256]{1,0:T(8,128)(2,1)} %param.14) | copy-start | bytes 393220
  248.7 178.2 %copy-start.10 = (bf16[1792,64]{0,1:T(8,128)(2,1)S(1)}, bf16[1792,64]{0,1:T(8,128)(2,1)}, u32[]{:S(2)}) copy-start(bf16[1792,64]{0,1:T(8,128)(2,1)} %param.21) | copy-start | bytes 688132
Sparse Core Ops, SparseCore 0:
  233.3 193.5 all-reduce.3
where the time goes:
time: 471 us; the launch traced here: 463 us
  blocking collectives  296 us (63%)
  matrix products  48.2 us (10%)
  waiting for transfers between devices  41 us (9%)
  other arithmetic  30 us (6%)
  local copies, waits for them, and re-layouts  18.1 us (4%)
  starting transfers between devices  15.1 us (3%)
  between operations  14.7 us (3%)
    pmax x1, blocking collectives, body(): global_cache_top = lax.pmax(assemble(cache_top), 'ctx')  144 us
    psum x1, blocking collectives, body(): summed, totals = lax.psum((cache_sums, cache_totals), 'ctx')  129 us
    psum x1, waiting for transfers between devices, body(): summed, totals = lax.psum((cache_sums, cache_totals), 'ctx')  41 us
    psum x1, blocking collectives, body(): draft_out = lax.psum(draft_terms, 'tp').astype(jnp.bfloat16)  23.4 us
    dot_general x4, matrix products, body(): jnp.dot(weights.astype(jnp.bfloat16), values, preferred_element_type=jnp....  22.5 us
    reduce_sum x4, other arithmetic, body(): cache_tot.append(jnp.sum(weights, axis=1).reshape(NODES, group))  18.4 us
    dot_general x4, matrix products, body(): jnp.einsum('qd,kd->qk', rows, keys, preferred_element_type=jnp.float32)  18.3 us
    all_to_all x1, starting transfers between devices, migrate(): lax.all_to_all(outgoing, 'ctx', split_axis=0, concat_axis=0, tiled=True)  15 us
  transfers between devices with their start and end apart: 2, of which 1 were waited for; matrix products, arithmetic and copies ran while one was open for 18% of the time, Pallas kernels for 0%

commit v1 on v0

v1 whole, which is shorter than its diff:
```python
import math

import jax
import jax.numpy as jnp
from jax import lax
from jax.experimental import pallas as pl
from jax.experimental.pallas import tpu as pltpu
from jax.sharding import PartitionSpec as P

MESH = pl.DeviceIdType.MESH
F32 = jnp.float32
BF16 = jnp.bfloat16

HD = 128
HEADS = 8
PAGE = 64
NODES = 64
SESS = 4
DD = 4096
XS, ZS, CS, TP = 4, 8, 2, 8
CHUNK = 512
FAR = -1e30
UNIT = math.log2(math.e) / math.sqrt(HD)
HALF = 896

F_CORE, F_X, F_Z = 0, 0, 3
G_CORE, G_Z, G_X, G_TP = 11, 11, 18, 21
A_CORE, A_XO, A_XW, A_ZO, A_ZW, A_FIN = 29, 32, 35, 38, 45, 53
M_CORE, M_X, M_Z = 54, 55, 61
COPIES = 61 + 8 * 7


def dot_nt(a, b):
    return lax.dot_general(a, b, (((1,), (1,)), ((), ())), preferred_element_type=F32)


def dot_nn(a, b):
    return jnp.dot(a, b, preferred_element_type=F32)


def merge(parts):
    n = parts[0][1].shape[0]
    spot = lax.broadcasted_iota(jnp.int32, (n, 128), 1)
    top = parts[0][1]
    for part in parts[1:]:
        top = jnp.maximum(top, part[1])
    total = None
    sums = [None] * 4
    for value, info in parts:
        factor = jnp.exp2(info - top)
        term = info * pltpu.roll(factor, 4, 1)
        total = term if total is None else total + term
        for i in range(4):
            term = value[i] * factor[:, i : i + 1]
            sums[i] = term if sums[i] is None else sums[i] + term
    return sums, jnp.where(spot < 4, top, jnp.where(spot < 8, total, 0.0))


def narrow(info):
    packed = info[0:8]
    for k in range(1, ZS):
        packed = packed + pltpu.roll(info[k * 8 : k * 8 + 8], 16 * k, 1)
    return packed


def widen(packed):
    spot = lax.broadcasted_iota(jnp.int32, (8, 128), 1)
    rows = [packed] + [pltpu.roll(packed, 128 - 16 * k, 1) for k in range(1, ZS)]
    return jnp.concatenate([jnp.where(spot < 8, row, 0.0) for row in rows], axis=0)


def kernel(
    kv, ps, q, tkv, parent, mc, states, accept, wg, wu, wd,
    attn_out, zin, draft_out,
    q2, bias, scores, mx, acc, tot,
    give0, give1, give2, give3, mine, core_in0, core_in1, core_in2, core_in3,
    xo0, xo1, xo2, xw0, xw1, xw2, xo_in, xw_in, zo, zw, zo_in, zw_in, fin, fin_in,
    f_out, f_core, f_b, f_x, f_s, f_z, h_own, h_z, h_s, h_x, h_t, h_c, hbf, d_own, d_in,
    to_core, own_pages, from_core, xin0, xin1, xin2, xin3, xin4, xin5,
    ssem, rsem, lsem,
):
    give = [give0, give1, give2, give3]
    core_in = [core_in0, core_in1, core_in2, core_in3]
    xo, xw = [xo0, xo1, xo2], [xw0, xw1, xw2]
    xin = [xin0, xin1, xin2, xin3, xin4, xin5]
    me = lax.axis_index("ctx")
    y = lax.axis_index("tp")
    x = me // 16
    z = lax.rem(me // 2, 8)
    c = lax.rem(me, 2)

    def ctx_at(px, pz, pc):
        return {"ctx": px * 16 + pz * 2 + pc}

    core_peer = ctx_at(x, z, 1 - c)

    def x_at(k):
        return lax.rem(x + k, XS)

    def z_at(k):
        return lax.rem(z + k, ZS)

    def x_peer(k):
        return ctx_at(x_at(k), z, c)

    def z_peer(k):
        return ctx_at(x, z_at(k), c)

    def y_peer(k):
        return {"tp": lax.rem(y + k, TP)}

    sent = []

    def send(src, dst, i, peer):
        cp = pltpu.make_async_remote_copy(
            src_ref=src, dst_ref=dst, send_sem=ssem.at[i], recv_sem=rsem.at[i],
            device_id=peer, device_id_type=MESH,
        )
        cp.start()
        sent.append(cp)
        return cp

    def arrive(cps):
        for cp in cps:
            cp.wait_recv()

    barrier = pltpu.get_barrier_semaphore()
    peers = [core_peer] + [z_peer(k) for k in range(1, ZS)]
    peers += [x_peer(k) for k in range(1, XS)] + [y_peer(k) for k in range(1, TP)]
    for peer in peers:
        pl.semaphore_signal(barrier, inc=1, device_id=peer, device_id_type=MESH)

    def pack(k, start):
        first = start
        second = start + mc[me, 2 * k]
        own = jnp.where(c == 0, first, second)
        other = jnp.where(c == 0, second, first)
        px, pz = k // ZS, lax.rem(k, ZS)
        own_pages[px, pz] = kv[own]
        to_core[px, pz] = kv[other]
        return second + mc[me, 2 * k + 1]

    lax.fori_loop(0, 32, pack, jnp.int32(0))

    sub = lax.broadcasted_iota(jnp.int32, (32, 256), 0)
    lane = lax.broadcasted_iota(jnp.int32, (32, 256), 1)
    row_of = jnp.zeros((32, 256), jnp.int32)
    for r in range(32):
        row_of = jnp.where(sub == r, accept[r // 8, r % 8] + (r // 8) * NODES, row_of)
    pick = jnp.where(lane == row_of, 1.0, 0.0).astype(BF16)
    chosen = dot_nt(pick, states[...])
    squares = jnp.broadcast_to(jnp.sum(chosen * chosen, axis=1, keepdims=True), (32, 256))
    chosen = chosen.astype(BF16)
    for half in range(2):
        gate = dot_nn(chosen, wg[:, half * HALF : (half + 1) * HALF])
        up = dot_nn(chosen, wu[:, half * HALF : (half + 1) * HALF])
        for px in range(XS):
            rows = slice(px * 8, px * 8 + 8)
            for j in range(7):
                cols = slice(j * 128, j * 128 + 128)
                f_out[half, px, j, :, 0:128] = gate[rows, cols]
                f_out[half, px, j, :, 128:256] = up[rows, cols]
            f_out[half, px, 7] = squares[rows, :]

    pl.semaphore_wait(barrier, len(peers))

    z_order = (1, 7, 2, 6, 3, 5, 4)
    m_z = []
    kept = []

    def send_group(src, group, lead=()):
        for k in z_order:
            m_z.append(
                send(src.at[(*lead, z_at(k))], zin.at[k, group], M_Z + group * 7 + k - 1, z_peer(k))
            )
        cp = pltpu.make_async_copy(src.at[(*lead, z)], zin.at[0, group], lsem.at[group])
        cp.start()
        kept.append(cp)

    f_cp = send(f_out.at[1 - c], f_core, F_CORE + 3, core_peer)
    m_core = send(to_core, from_core, M_CORE, core_peer)
    send_group(own_pages, 0, (x,))

    for s in range(SESS):
        for h in range(HEADS):
            q2[s, h * NODES : (h + 1) * NODES, :] = q[
                s * NODES : (s + 1) * NODES, h * HD : (h + 1) * HD
            ]
    lane1 = lax.broadcasted_iota(jnp.int32, (1, 128), 1)
    for t in range(32):
        session = jnp.where(lane1 < PAGE, ps[2 * t], ps[2 * t + 1])
        for s in range(SESS):
            bias[s, :, t * 128 : (t + 1) * 128] = jnp.where(session == s, 0.0, FAR).astype(F32)

    m_x = {}

    def send_x(k, part):
        src = own_pages if part == 0 else from_core
        m_x[k, part] = send(
            src.at[x_at(k)], xin[(k - 1) * 2 + part], M_X + (k - 1) * 2 + part, x_peer(k)
        )

    def forward(k, part):
        m_x[k, part].wait_recv()
        send_group(xin[(k - 1) * 2 + part], k * 2 + part)

    def attend(n, k):
        s = x_at(k)
        rows = q2[s]
        mx[...] = jnp.full((512, 128), FAR, F32)

        def first(t, carry):
            at = pl.ds(pl.multiple_of(t * CHUNK, CHUNK), CHUNK)
            pages = pl.ds(t * (CHUNK // PAGE), CHUNK // PAGE)
            keys = kv[pages, :, 0:HD].reshape(CHUNK, HD)
            part = dot_nt(rows, keys) + bias[s, :, at]
            scores[:, at] = part
            top = mx[...]
            for i in range(CHUNK // 128):
                top = jnp.maximum(top, part[:, i * 128 : (i + 1) * 128])
            mx[...] = top
            return carry

        lax.fori_loop(0, 4096 // CHUNK, first, 0)
        top = jnp.max(mx[...], axis=1, keepdims=True) * UNIT
        mx[...] = jnp.broadcast_to(top, (512, 128))
        acc[...] = jnp.zeros((512, 128), F32)
        tot[...] = jnp.zeros((512, 128), F32)

        def second(t, carry):
            at = pl.ds(pl.multiple_of(t * CHUNK, CHUNK), CHUNK)
            pages = pl.ds(t * (CHUNK // PAGE), CHUNK // PAGE)
            weight = jnp.exp2(scores[:, at] * UNIT - top)
            part = weight[:, 0:128]
            for i in range(1, CHUNK // 128):
                part = part + weight[:, i * 128 : (i + 1) * 128]
            tot[...] = tot[...] + part
            values = kv[pages, :, HD : 2 * HD].reshape(CHUNK, HD)
            acc[...] = acc[...] + dot_nn(weight.astype(BF16), values)
            return carry

        lax.fori_loop(0, 4096 // CHUNK, second, 0)
        tot[...] = jnp.broadcast_to(jnp.sum(tot[...], axis=1, keepdims=True), (512, 128))
        spot = lax.broadcasted_iota(jnp.int32, (NODES, 128), 1)
        for part, group in ((give[n], 1 - c), (mine.at[n], c)):
            info = jnp.zeros((NODES, 128), F32)
            for i in range(4):
                at = pl.ds(pl.multiple_of(group * 256 + i * NODES, NODES), NODES)
                part[i] = acc[at, :]
                info = jnp.where(spot == i, mx[at, :], info)
                info = jnp.where(spot == 4 + i, tot[at, :], info)
            part[4] = info
        return send(give[n], core_in[n], A_CORE + n if n < 3 else A_FIN - 1, core_peer)

    def part_of(ref):
        return [ref[i] for i in range(4)], ref[4]

    a_x = []

    def join(n, k, cp):
        cp.wait_recv()
        sums, info = merge([part_of(mine.at[n]), part_of(core_in[n])])
        if k == 0:
            for i in range(4):
                mine[n, i] = sums[i]
            mine[n, 4] = info
            return
        for i in range(4):
            xo[n][i * NODES : (i + 1) * NODES, :] = sums[i].astype(BF16)
        xw[n][...] = narrow(info)
        a_x.append(send(xo[n], xo_in.at[k - 1], A_XO + k - 1, x_peer(k)))
        a_x.append(send(xw[n], xw_in.at[k - 1], A_XW + k - 1, x_peer(k)))

    a0 = attend(0, 1)

    f_cp.wait_recv()
    for px in range(XS):
        f_b[px] = (f_core[px] + f_out[c, px]).reshape(64, 256)
    f_xs = [send(f_b.at[x_at(k)], f_x.at[k - 1], F_X + k - 1, x_peer(k)) for k in range(1, XS)]
    send_x(1, 0)
    send_x(3, 0)
    m_core.wait_recv()
    send_group(from_core, 1, (x,))
    join(0, 1, a0)
    send_x(1, 1)
    send_x(3, 1)

    a1 = attend(1, 3)

    arrive(f_xs)
    whole = f_b[x]
    for k in range(XS - 1):
        whole = whole + f_x[k]
    for j in range(ZS):
        f_s[j, :, 0:256] = whole[j * 8 : j * 8 + 8]
        f_s[j, :, 256:384] = whole[56:64, 0:128]
    f_zs = [send(f_s.at[z_at(k)], f_z.at[k - 1], F_Z + k, z_peer(k)) for k in range(1, ZS)]
    join(1, 3, a1)
    send_x(2, 0)

    a2 = attend(2, 2)

    arrive(f_zs)
    whole = f_s[z]
    for k in range(ZS - 1):
        whole = whole + f_z[k]
    inverse = lax.rsqrt(whole[:, 256:384] / DD + 1e-05)
    gate = inverse * whole[:, 0:128]
    up = inverse * whole[:, 128:256]
    hidden = gate / (1.0 + jnp.exp(-gate)) * up
    h_own[...] = hidden.astype(BF16).astype(F32)
    g_zs = [send(h_own, h_z.at[k - 1], G_Z + k, z_peer(k)) for k in range(1, ZS)]
    join(2, 2, a2)
    send_x(2, 1)
    forward(1, 0)
    forward(3, 0)

    a3 = attend(3, 0)

    arrive(g_zs)
    for j in range(7):
        slot = lax.rem(z - j + ZS, ZS)
        h_s[j] = jnp.where(slot == 0, h_own[...], h_z[jnp.maximum(slot - 1, 0)])
    g_xs = [send(h_s, h_x.at[k - 1], G_X + k, x_peer(k)) for k in range(1, XS)]
    join(3, 0, a3)
    forward(1, 1)
    forward(3, 1)

    link_at = lax.broadcasted_iota(jnp.int32, (NODES, NODES), 0)
    node_at = lax.broadcasted_iota(jnp.int32, (NODES, NODES), 1)
    link = jnp.where((parent[pl.ds(x, 1), :] == link_at) | (link_at == node_at), 1.0, 0.0)
    for repeat in range(6):
        link = jnp.minimum(dot_nn(link.astype(BF16), link.astype(BF16)), 1.0)
    own_row = lax.broadcasted_iota(jnp.int32, (32, NODES), 0)
    own_node = lax.broadcasted_iota(jnp.int32, (32, NODES), 1)
    own = jnp.where(own_node == z * 8 + lax.rem(own_row, 8), 1.0, 0.0).astype(BF16)
    reach = dot_nt(own, link.astype(BF16)) > 0.5
    block = pl.ds(pl.multiple_of(x * NODES, NODES), NODES)
    picks = []
    for i in range(4):
        rows = q2[x, pl.ds(pl.multiple_of(c * 256 + i * NODES, NODES), NODES), :]
        picks.append(dot_nn(own[0:8], rows))
    q_own = jnp.concatenate(picks, axis=0).astype(BF16)
    branch = jnp.where(reach, dot_nt(q_own, tkv[block, 0:HD]) * UNIT, FAR)
    tree_top = jnp.max(branch, axis=1, keepdims=True)
    weight = jnp.exp2(branch - tree_top)
    tree_total = jnp.sum(weight, axis=1, keepdims=True)
    tree_sum = dot_nn(weight.astype(BF16), tkv[block, HD : 2 * HD])
    spot8 = lax.broadcasted_iota(jnp.int32, (8, 128), 1)
    info = jnp.zeros((8, 128), F32)
    for i in range(4):
        at = slice(i * 8, i * 8 + 8)
        info = jnp.where(spot8 == i, tree_top[at], info)
        info = jnp.where(spot8 == 4 + i, tree_total[at], info)
    tree_part = ([tree_sum[i * 8 : i * 8 + 8] for i in range(4)], info)

    arrive(g_xs)
    for px in range(XS):
        slot = lax.rem(x - px + XS, XS)
        h_t[px] = jnp.where(slot == 0, h_s[...], h_x[jnp.maximum(slot - 1, 0)])
    g_c = send(h_t, h_c, G_CORE, core_peer)

    arrive(a_x)
    parts = [part_of(mine.at[3])]
    for k in range(XS - 1):
        value = xo_in[k].astype(F32)
        parts.append(
            ([value[i * NODES : (i + 1) * NODES] for i in range(4)], widen(xw_in[k]))
        )
    sums, info = merge(parts)
    for k in range(ZS):
        at = slice(k * 8, k * 8 + 8)
        zo[k] = jnp.concatenate([sums[i][at] for i in range(4)], axis=0).astype(BF16)
        zw[k] = info[at]
    a_zs = []
    for k in range(1, ZS):
        a_zs.append(send(zo.at[z_at(k)], zo_in.at[k - 1], A_ZO + k - 1, z_peer(k)))
        a_zs.append(send(zw.at[z_at(k)], zw_in.at[k - 1], A_ZW + k - 1, z_peer(k)))

    g_c.wait_recv()
    for g in range(2):
        for j in range(7):
            at = slice(g * HALF + j * 128, g * HALF + j * 128 + 128)
            tile = jnp.where(c == g, h_t[:, j].reshape(32, 128), h_c[:, j].reshape(32, 128))
            hbf[:, at] = tile.astype(BF16)
    terms = dot_nt(hbf[...], wd[...])
    d_own[...] = jnp.concatenate([terms[0:16], terms[16:32]], axis=1)
    d_cps = [send(d_own, d_in.at[k - 1], G_TP + k, y_peer(k)) for k in range(1, TP)]
    forward(2, 0)
    forward(2, 1)

    def four(value):
        return [value[i * 8 : i * 8 + 8] for i in range(4)]

    arrive(a_zs)
    parts = [tree_part, (four(zo[z].astype(F32)), zw[z])]
    parts += [(four(zo_in[k].astype(F32)), zw_in[k]) for k in range(ZS - 1)]
    sums, info = merge(parts)
    for i in range(4):
        fin[i] = sums[i] / info[:, 4 + i : 5 + i]
    last = send(fin, fin_in, A_FIN, core_peer)
    arrive(d_cps)
    done = None
    for j in range(TP):
        slot = lax.rem(y - j + TP, TP)
        term = jnp.where(slot == 0, d_own[...], d_in[jnp.maximum(slot - 1, 0)])
        done = term if done is None else done + term
    draft_out[...] = jnp.concatenate([done[:, 0:64], done[:, 64:128]], axis=0).astype(BF16)
    last.wait_recv()
    for h in range(HEADS):
        tile = jnp.where(c == h // 4, fin[h % 4], fin_in[h % 4])
        attn_out[:, h * HD : (h + 1) * HD] = jnp.where(c == 0, tile[0:4], tile[4:8]).astype(BF16)

    arrive(m_z)
    for cp in kept:
        cp.wait()
    for cp in sent:
        cp.wait_send()


def place(attn, pages, draft, mc, attn_out, arrived, draft_out, after):
    me = lax.axis_index("ctx")

    def back(i, carry):
        s = 63 - i
        carry = jnp.where(mc[s, me] > 0, s, carry)
        after[s] = carry
        return carry

    after[64] = 64
    lax.fori_loop(0, 64, back, jnp.int32(64))

    def one(j, s):
        source = jnp.minimum(s, 63)
        kz = lax.rem(me // 2 - source // 2 + 64, ZS)
        kx = lax.rem(me // 16 - source // 16 + XS, XS)
        kc = lax.rem(me + source, 2)
        page = pages[kz, kx * 2 + kc]
        page = jnp.where(s < 64, page, jnp.zeros_like(page))
        arrived[pl.ds(pl.multiple_of(j * PAGE, PAGE), PAGE), :] = page
        return after[jnp.minimum(s + 1, 64)]

    lax.fori_loop(0, 32, one, after[0])
    attn_out[...] = attn[...]
    draft_out[...] = draft[...]


def body(
    kv_cache, page_session, queries, tree_kv, tree_parent, move_count,
    draft_states, accept_node, w_gate, w_up, w_down,
):
    vmem = pl.BlockSpec(memory_space=pltpu.VMEM)
    smem = pl.BlockSpec(memory_space=pltpu.SMEM)
    hbm = pl.BlockSpec(memory_space=pl.ANY)
    scratch = [
        pltpu.VMEM((SESS, 512, 128), BF16),
        pltpu.VMEM((SESS, 1, 4096), F32),
        pltpu.VMEM((512, 4096), F32),
        pltpu.VMEM((512, 128), F32),
        pltpu.VMEM((512, 128), F32),
        pltpu.VMEM((512, 128), F32),
        *[pltpu.VMEM((5, NODES, 128), F32)] * 4,
        pltpu.VMEM((4, 5, NODES, 128), F32),
        *[pltpu.VMEM((5, NODES, 128), F32)] * 4,
        *[pltpu.VMEM((256, 128), BF16)] * 3,
        *[pltpu.VMEM((8, 128), F32)] * 3,
        pltpu.VMEM((3, 256, 128), BF16),
        pltpu.VMEM((3, 8, 128), F32),
        pltpu.VMEM((ZS, 32, 128), BF16),
        pltpu.VMEM((ZS, 8, 128), F32),
        pltpu.VMEM((ZS - 1, 32, 128), BF16),
        pltpu.VMEM((ZS - 1, 8, 128), F32),
        pltpu.VMEM((4, 8, 128), F32),
        pltpu.VMEM((4, 8, 128), F32),
        pltpu.VMEM((2, XS, 8, 8, 256), F32),
        pltpu.VMEM((XS, 8, 8, 256), F32),
        pltpu.VMEM((XS, 64, 256), F32),
        pltpu.VMEM((XS - 1, 64, 256), F32),
        pltpu.VMEM((ZS, 8, 384), F32),
        pltpu.VMEM((ZS - 1, 8, 384), F32),
        pltpu.VMEM((8, 128), F32),
        pltpu.VMEM((ZS - 1, 8, 128), F32),
        pltpu.VMEM((7, 8, 128), F32),
        pltpu.VMEM((XS - 1, 7, 8, 128), F32),
        pltpu.VMEM((XS, 7, 8, 128), F32),
        pltpu.VMEM((XS, 7, 8, 128), F32),
        pltpu.VMEM((32, 1792), BF16),
        pltpu.VMEM((16, 128), F32),
        pltpu.VMEM((TP - 1, 16, 128), F32),
        pltpu.VMEM((XS, ZS, PAGE, 256), BF16),
        pltpu.VMEM((XS, ZS, PAGE, 256), BF16),
        pltpu.VMEM((XS, ZS, PAGE, 256), BF16),
        *[pltpu.VMEM((ZS, PAGE, 256), BF16)] * 6,
        pltpu.SemaphoreType.DMA((COPIES,)),
        pltpu.SemaphoreType.DMA((COPIES,)),
        pltpu.SemaphoreType.DMA((8,)),
    ]
    attn, pages, draft = pl.pallas_call(
        kernel,
        out_shape=(
            jax.ShapeDtypeStruct((4, 1024), BF16),
            jax.ShapeDtypeStruct((ZS, 8, PAGE, 256), BF16),
            jax.ShapeDtypeStruct((32, 64), BF16),
        ),
        in_specs=[vmem, smem, vmem, vmem, vmem, smem, vmem, smem, vmem, vmem, vmem],
        out_specs=(vmem, hbm, vmem),
        scratch_shapes=scratch,
        compiler_params=pltpu.CompilerParams(
            collective_id=0, has_side_effects=True, vmem_limit_bytes=56 * 1024 * 1024
        ),
        cost_estimate=pl.CostEstimate(
            flops=4 * 2048 * 4096 * 128, bytes_accessed=5 << 20, transcendentals=2048 * 4096
        ),
    )(
        kv_cache.reshape(64, PAGE, 256), page_session, queries, tree_kv, tree_parent, move_count,
        draft_states.T, accept_node, w_gate, w_up, w_down.T,
    )
    return pl.pallas_call(
        place,
        out_shape=(
            jax.ShapeDtypeStruct((4, 1024), BF16),
            jax.ShapeDtypeStruct((32 * PAGE, 256), BF16),
            jax.ShapeDtypeStruct((32, 64), BF16),
        ),
        in_specs=[vmem, vmem, vmem, smem],
        out_specs=(vmem, vmem, vmem),
        scratch_shapes=[pltpu.SMEM((65,), jnp.int32)],
        compiler_params=pltpu.CompilerParams(vmem_limit_bytes=16 * 1024 * 1024),
    )(attn, pages, draft, move_count)


def solution(mesh):
    placed = (
        P("ctx", "tp"),
        P("ctx"),
        P(None, "tp"),
        P(None, "tp"),
        P(),
        P(),
        P(None, "ctx"),
        P(),
        P("ctx", "tp"),
        P("ctx", "tp"),
        P("tp", "ctx"),
    )
    return jax.shard_map(
        body,
        mesh=mesh,
        in_specs=placed,
        out_specs=(P("ctx", "tp"), P("ctx", "tp"), P(None, "ctx")),
        check_vma=False,
    )
```

time: 471 us -> 86.9 us (0.18); the launches traced: 463 us -> 86.6 us
  blocking collectives: 296 us -> 0 us
  Pallas kernels: 0 us -> 83 us
  matrix products: 48.2 us -> 0 us
  waiting for transfers between devices: 41 us -> 0 us
  other arithmetic: 30 us -> 0 us
  local copies, waits for them, and re-layouts: 18.1 us -> 2.98 us
  starting transfers between devices: 15.1 us -> 0 us
  between operations: 14.7 us -> 0.67 us
    psum x2 -> x0, blocking collectives: 152 us -> none  [the longest x1 129 us: body(): summed, totals = lax.psum((cache_sums, cache_totals), 'ctx')]
    pmax x1 -> x0, blocking collectives: 144 us -> none  [body(): global_cache_top = lax.pmax(assemble(cache_top), 'ctx')]
    pallas_call x0 -> x2, Pallas kernels: none -> 83 us  [the longest x1 79.4 us: body(): pl.pallas_call(kernel, out_shape=(jax.ShapeDtypeStruct((4, 1024), BF16),...]
    dot_general x26 -> x0, matrix products: 48.2 us -> none  [the longest x4 22.5 us: body(): jnp.dot(weights.astype(jnp.bfloat16), values, preferred_element_type=jnp....]
    psum x1 -> x0, waiting for transfers between devices: 41 us -> none  [body(): summed, totals = lax.psum((cache_sums, cache_totals), 'ctx')]
    reduce_sum x10 -> x0, other arithmetic: 18.9 us -> none  [the longest x4 18.4 us: body(): cache_tot.append(jnp.sum(weights, axis=1).reshape(NODES, group))]
    all_to_all x1 -> x0, starting transfers between devices: 15 us -> none  [migrate(): lax.all_to_all(outgoing, 'ctx', split_axis=0, concat_axis=0, tiled=True)]
    reshape x51 -> x0, local copies, waits for them, and re-layouts: 7.3 us -> none  [the longest x4 3.74 us: body(): cache_acc.append(jnp.dot(weights.astype(jnp.bfloat16), values, preferred_...]
  transfers between devices with their start and end apart: 2 -> 0, of which waited for: 1 -> 0; matrix products, arithmetic and copies ran while one was open for 18% -> 0% of each run, Pallas kernels for 0% -> 0%
where the time goes in v1:
time: 86.9 us; the launch traced here: 86.6 us
  Pallas kernels  83 us (96%)
  local copies, waits for them, and re-layouts  2.98 us (3%)
    pallas_call x1, Pallas kernels, body(): pl.pallas_call(kernel, out_shape=(jax.ShapeDtypeStruct((4, 1024), BF16),...  79.4 us
    pallas_call x1, Pallas kernels, body(): pl.pallas_call(place, out_shape=(jax.ShapeDtypeStruct((4, 1024), BF16), j...  3.52 us
    unnamed x8, local copies, waits for them, and re-layouts  2.98 us

profile of v1, /device:TPU:1, one launch (start us, length us, event | category | flops | bytes accessed | tf_op | source)
XLA Modules:
  0.0 86.6 jit_solution(10577078779061037781)
XLA Ops:
  0.6 0.0 copy-start.1
  0.6 79.4 %shard_map.130 = (bf16[4,1024]{1,0:T(4,128)(2,1)}, bf16[8,8,64,256]{3,2,1,0:T(8,128)(2,1)}, bf16[32,64]{1,0:T(8,128)(2,1)}) custom-call(bf16[64,64,256]{2,1,0:T(8,128)(2,1)} %bitcast.3, s32[64]{0:T(128)} %ps.1, bf16[256,1024]{1,0:T(8,128)(2,1)} %q.1, bf16[256,256]{1,0:T(8,128)(2,1)} %tkv.1, s32[4,64]{1,0:T(4,128)} %parent.1, s32[64,64]{1,0:T(8,128)} %mc.3, ...), custom_call_target="tpu_custom_call" | custom-call | flops 4294967296 | bytes 5242880 | tf_op jit(solution)/shard_map/pallas_call | solution.py:498
  80.1 0.0 copy-done.1
  80.1 0.0 copy-start
  80.1 1.6 %copy-done = bf16[8,8,64,256]{3,2,1,0:T(8,128)(2,1)S(1)} copy-done((bf16[8,8,64,256]{3,2,1,0:T(8,128)(2,1)S(1)}, bf16[8,8,64,256]{3,2,1,0:T(8,128)(2,1)}, u32[]{:S(2)}) %copy-start) | copy-done | bytes 2097176
  81.7 0.0 copy-start.2
  81.7 0.7 copy-done.2
  82.4 0.0 copy-start.3
  82.4 0.7 copy-done.3
  83.1 3.5 %shard_map.131 = (bf16[4,1024]{1,0:T(4,128)(2,1)}, bf16[2048,256]{1,0:T(8,128)(2,1)}, bf16[32,64]{1,0:T(8,128)(2,1)}) custom-call(bf16[4,1024]{1,0:T(4,128)(2,1)S(1)} %copy-done.2, bf16[8,8,64,256]{3,2,1,0:T(8,128)(2,1)S(1)} %copy-done, bf16[32,64]{1,0:T(8,128)(2,1)S(1)} %copy-done.3, s32[64,64]{1,0:T(8,128)S(1)} %copy-done.1), custom_call_target="tpu_custom_call" | custom-call | tf_op jit(solution)/shard_map/pallas_call | solution.py:518
Async XLA Ops:
  0.6 79.5 %copy-start.1 = (s32[64,64]{1,0:T(8,128)S(1)}, s32[64,64]{1,0:T(8,128)}, u32[]{:S(2)}) copy-start(s32[64,64]{1,0:T(8,128)} %mc.3) | copy-start | bytes 49156
  80.1 1.6 %copy-start = (bf16[8,8,64,256]{3,2,1,0:T(8,128)(2,1)S(1)}, bf16[8,8,64,256]{3,2,1,0:T(8,128)(2,1)}, u32[]{:S(2)}) copy-start(bf16[8,8,64,256]{3,2,1,0:T(8,128)(2,1)} %get-tuple-element.7.pages) | copy-start | bytes 6291460
  81.7 0.7 copy-start.2
  82.4 0.7 copy-start.3

commit v2 on v1

--- a/solution.py
+++ b/solution.py
@@ -69,20 +69,33 @@
     return jnp.concatenate([jnp.where(spot < 8, row, 0.0) for row in rows], axis=0)
 
 
+def split(info):
+    high = info.astype(BF16).astype(F32)
+    rest = info - high
+    middle = rest.astype(BF16).astype(F32)
+    both = high + pltpu.roll(middle, 8, 1)
+    return jnp.concatenate([both, rest - middle], axis=0).astype(BF16)
+
+
+def joined(tile):
+    tile = tile.astype(F32)
+    return tile[0:8] + pltpu.roll(tile[0:8], 120, 1) + tile[8:16]
+
+
 def kernel(
-    kv, ps, q, tkv, parent, mc, states, accept, wg, wu, wd,
-    attn_out, zin, draft_out,
+    kv_h, ps, q_h, tkv_h, parent, mc, states, accept, wg_h, wu_h, wd_h, moves,
+    attn_out, zin, draft_out, order,
     q2, bias, scores, mx, acc, tot,
     give0, give1, give2, give3, mine, core_in0, core_in1, core_in2, core_in3,
-    xo0, xo1, xo2, xw0, xw1, xw2, xo_in, xw_in, zo, zw, zo_in, zw_in, fin, fin_in,
+    xo0, xo1, xo2, xo_in, zo, zo_in, fin, fin_in,
     f_out, f_core, f_b, f_x, f_s, f_z, h_own, h_z, h_s, h_x, h_t, h_c, hbf, d_own, d_in,
-    to_core, own_pages, from_core, xin0, xin1, xin2, xin3, xin4, xin5,
-    ssem, rsem, lsem,
+    to_core, own_pages, from_core, xin0, xin1, xin2,
+    kv, q, tkv, wg, wu, wd, blank, ssem, rsem, lsem, isem,
 ):
     give = [give0, give1, give2, give3]
     core_in = [core_in0, core_in1, core_in2, core_in3]
-    xo, xw = [xo0, xo1, xo2], [xw0, xw1, xw2]
-    xin = [xin0, xin1, xin2, xin3, xin4, xin5]
+    xo = [xo0, xo1, xo2]
+    xin = [xin0, xin1, xin2]
     me = lax.axis_index("ctx")
     y = lax.axis_index("tp")
     x = me // 16
@@ -130,17 +143,11 @@
     for peer in peers:
         pl.semaphore_signal(barrier, inc=1, device_id=peer, device_id_type=MESH)
 
-    def pack(k, start):
-        first = start
-        second = start + mc[me, 2 * k]
-        own = jnp.where(c == 0, first, second)
-        other = jnp.where(c == 0, second, first)
-        px, pz = k // ZS, lax.rem(k, ZS)
-        own_pages[px, pz] = kv[own]
-        to_core[px, pz] = kv[other]
-        return second + mc[me, 2 * k + 1]
-
-    lax.fori_loop(0, 32, pack, jnp.int32(0))
+    loads = []
+    for src, dst in ((wg_h, wg), (wu_h, wu), (kv_h, kv), (q_h, q), (tkv_h, tkv), (wd_h, wd)):
+        cp = pltpu.make_async_copy(src, dst, isem.at[len(loads)])
+        cp.start()
+        loads.append(cp)
 
     sub = lax.broadcasted_iota(jnp.int32, (32, 256), 0)
     lane = lax.broadcasted_iota(jnp.int32, (32, 256), 1)
@@ -151,6 +158,8 @@
     chosen = dot_nt(pick, states[...])
     squares = jnp.broadcast_to(jnp.sum(chosen * chosen, axis=1, keepdims=True), (32, 256))
     chosen = chosen.astype(BF16)
+    loads[0].wait()
+    loads[1].wait()
     for half in range(2):
         gate = dot_nn(chosen, wg[:, half * HALF : (half + 1) * HALF])
         up = dot_nn(chosen, wu[:, half * HALF : (half + 1) * HALF])
@@ -162,11 +171,28 @@
                 f_out[half, px, j, :, 128:256] = up[rows, cols]
             f_out[half, px, 7] = squares[rows, :]
 
+    def pack(k, start):
+        first = start
+        second = start + mc[me, 2 * k]
+        own = jnp.where(c == 0, first, second)
+        other = jnp.where(c == 0, second, first)
+        px, pz = k // ZS, lax.rem(k, ZS)
+        own_pages[px, pz] = kv[own]
+        to_core[px, pz] = kv[other]
+        return second + mc[me, 2 * k + 1]
+
+    loads[2].wait()
+    lax.fori_loop(0, 32, pack, jnp.int32(0))
+
     pl.semaphore_wait(barrier, len(peers))
 
     z_order = (1, 7, 2, 6, 3, 5, 4)
     m_z = []
     kept = []
+    blank[...] = jnp.zeros((PAGE, 256), BF16)
+    cp = pltpu.make_async_copy(blank, zin.at[ZS, 0], lsem.at[8])
+    cp.start()
+    kept.append(cp)
 
     def send_group(src, group, lead=()):
         for k in z_order:
@@ -181,6 +207,7 @@
     m_core = send(to_core, from_core, M_CORE, core_peer)
     send_group(own_pages, 0, (x,))
 
+    loads[3].wait()
     for s in range(SESS):
         for h in range(HEADS):
             q2[s, h * NODES : (h + 1) * NODES, :] = q[
@@ -197,12 +224,12 @@
     def send_x(k, part):
         src = own_pages if part == 0 else from_core
         m_x[k, part] = send(
-            src.at[x_at(k)], xin[(k - 1) * 2 + part], M_X + (k - 1) * 2 + part, x_peer(k)
+            src.at[x_at(k)], xin[k - 1].at[part], M_X + (k - 1) * 2 + part, x_peer(k)
         )
 
     def forward(k, part):
         m_x[k, part].wait_recv()
-        send_group(xin[(k - 1) * 2 + part], k * 2 + part)
+        send_group(xin[k - 1], k * 2 + part, (part,))
 
     def attend(n, k):
         s = x_at(k)
@@ -267,11 +294,8 @@
             return
         for i in range(4):
             xo[n][i * NODES : (i + 1) * NODES, :] = sums[i].astype(BF16)
-        xw[n][...] = narrow(info)
+        xo[n][256:272, :] = split(narrow(info))
         a_x.append(send(xo[n], xo_in.at[k - 1], A_XO + k - 1, x_peer(k)))
-        a_x.append(send(xw[n], xw_in.at[k - 1], A_XW + k - 1, x_peer(k)))
-
-    a0 = attend(0, 1)
 
     f_cp.wait_recv()
     for px in range(XS):
@@ -281,11 +305,12 @@
     send_x(3, 0)
     m_core.wait_recv()
     send_group(from_core, 1, (x,))
-    join(0, 1, a0)
     send_x(1, 1)
     send_x(3, 1)
 
-    a1 = attend(1, 3)
+    send_x(2, 0)
+    send_x(2, 1)
+    a0 = attend(0, 1)
 
     arrive(f_xs)
     whole = f_b[x]
@@ -295,10 +320,11 @@
         f_s[j, :, 0:256] = whole[j * 8 : j * 8 + 8]
         f_s[j, :, 256:384] = whole[56:64, 0:128]
     f_zs = [send(f_s.at[z_at(k)], f_z.at[k - 1], F_Z + k, z_peer(k)) for k in range(1, ZS)]
-    join(1, 3, a1)
-    send_x(2, 0)
-
-    a2 = attend(2, 2)
+    join(0, 1, a0)
+    forward(1, 0)
+    forward(3, 0)
+
+    a1 = attend(1, 3)
 
     arrive(f_zs)
     whole = f_s[z]
@@ -310,21 +336,37 @@
     hidden = gate / (1.0 + jnp.exp(-gate)) * up
     h_own[...] = hidden.astype(BF16).astype(F32)
     g_zs = [send(h_own, h_z.at[k - 1], G_Z + k, z_peer(k)) for k in range(1, ZS)]
+    join(1, 3, a1)
+    forward(1, 1)
+    forward(3, 1)
+
+    a2 = attend(2, 2)
+
     join(2, 2, a2)
-    send_x(2, 1)
-    forward(1, 0)
-    forward(3, 0)
-
-    a3 = attend(3, 0)
-
+    forward(2, 0)
     arrive(g_zs)
     for j in range(7):
         slot = lax.rem(z - j + ZS, ZS)
         h_s[j] = jnp.where(slot == 0, h_own[...], h_z[jnp.maximum(slot - 1, 0)])
     g_xs = [send(h_s, h_x.at[k - 1], G_X + k, x_peer(k)) for k in range(1, XS)]
+
+    a3 = attend(3, 0)
+
     join(3, 0, a3)
-    forward(1, 1)
-    forward(3, 1)
+    forward(2, 1)
+
+    shard = lax.broadcasted_iota(jnp.int32, (64, 64), 0)
+    other = lax.broadcasted_iota(jnp.int32, (64, 64), 1)
+    count = jnp.sum(jnp.where(other == me, moves[...], 0).astype(F32), axis=1, keepdims=True)
+    count = jnp.broadcast_to(count, (64, 128))
+    rank = dot_nn(jnp.where(other < shard, 1.0, 0.0).astype(BF16), count.astype(BF16))
+    shard = lax.broadcasted_iota(jnp.int32, (64, 128), 0)
+    place_of = lax.broadcasted_iota(jnp.int32, (64, 128), 1).astype(F32)
+    slot = lax.rem(z - lax.rem(shard // 2, ZS) + ZS, ZS) * 8
+    slot = slot + lax.rem(x - shard // 16 + XS, XS) * 2 + lax.rem(c + shard, 2)
+    hit = (rank == place_of) & (count > 0.5)
+    found = jnp.sum(jnp.where(hit, slot.astype(F32) - 64.0, 0.0), axis=0, keepdims=True) + 64.0
+    order[...] = jnp.broadcast_to(found, (8, 128)).astype(jnp.int32)
 
     link_at = lax.broadcasted_iota(jnp.int32, (NODES, NODES), 0)
     node_at = lax.broadcasted_iota(jnp.int32, (NODES, NODES), 1)
@@ -335,6 +377,8 @@
     own_node = lax.broadcasted_iota(jnp.int32, (32, NODES), 1)
     own = jnp.where(own_node == z * 8 + lax.rem(own_row, 8), 1.0, 0.0).astype(BF16)
     reach = dot_nt(own, link.astype(BF16)) > 0.5
+    loads[4].wait()
+    loads[5].wait()
     block = pl.ds(pl.multiple_of(x * NODES, NODES), NODES)
     picks = []
     for i in range(4):
@@ -363,19 +407,18 @@
     arrive(a_x)
     parts = [part_of(mine.at[3])]
     for k in range(XS - 1):
-        value = xo_in[k].astype(F32)
+        value = xo_in[k, 0:256].astype(F32)
         parts.append(
-            ([value[i * NODES : (i + 1) * NODES] for i in range(4)], widen(xw_in[k]))
+            ([value[i * NODES : (i + 1) * NODES] for i in range(4)], widen(joined(xo_in[k, 256:272])))
         )
     sums, info = merge(parts)
     for k in range(ZS):
         at = slice(k * 8, k * 8 + 8)
-        zo[k] = jnp.concatenate([sums[i][at] for i in range(4)], axis=0).astype(BF16)
-        zw[k] = info[at]
+        zo[k, 0:32] = jnp.concatenate([sums[i][at] for i in range(4)], axis=0).astype(BF16)
+        zo[k, 32:48] = split(info[at])
     a_zs = []
     for k in range(1, ZS):
         a_zs.append(send(zo.at[z_at(k)], zo_in.at[k - 1], A_ZO + k - 1, z_peer(k)))
-        a_zs.append(send(zw.at[z_at(k)], zw_in.at[k - 1], A_ZW + k - 1, z_peer(k)))
 
     g_c.wait_recv()
     for g in range(2):
@@ -386,15 +429,14 @@
     terms = dot_nt(hbf[...], wd[...])
     d_own[...] = jnp.concatenate([terms[0:16], terms[16:32]], axis=1)
     d_cps = [send(d_own, d_in.at[k - 1], G_TP + k, y_peer(k)) for k in range(1, TP)]
-    forward(2, 0)
-    forward(2, 1)
-
-    def four(value):
-        return [value[i * 8 : i * 8 + 8] for i in range(4)]
+
+    def four(tile):
+        value = tile[0:32].astype(F32)
+        info = jnp.where(spot8 < 8, joined(tile[32:48]), 0.0)
+        return [value[i * 8 : i * 8 + 8] for i in range(4)], info
 
     arrive(a_zs)
-    parts = [tree_part, (four(zo[z].astype(F32)), zw[z])]
-    parts += [(four(zo_in[k].astype(F32)), zw_in[k]) for k in range(ZS - 1)]
+    parts = [tree_part, four(zo[z])] + [four(zo_in[k]) for k in range(ZS - 1)]
     sums, info = merge(parts)
     for i in range(4):
         fin[i] = sums[i] / info[:, 4 + i : 5 + i]
@@ -418,31 +460,20 @@
         cp.wait_send()
 
 
-def place(attn, pages, draft, mc, attn_out, arrived, draft_out, after):
-    me = lax.axis_index("ctx")
-
-    def back(i, carry):
-        s = 63 - i
-        carry = jnp.where(mc[s, me] > 0, s, carry)
-        after[s] = carry
-        return carry
-
-    after[64] = 64
-    lax.fori_loop(0, 64, back, jnp.int32(64))
-
-    def one(j, s):
-        source = jnp.minimum(s, 63)
-        kz = lax.rem(me // 2 - source // 2 + 64, ZS)
-        kx = lax.rem(me // 16 - source // 16 + XS, XS)
-        kc = lax.rem(me + source, 2)
-        page = pages[kz, kx * 2 + kc]
-        page = jnp.where(s < 64, page, jnp.zeros_like(page))
-        arrived[pl.ds(pl.multiple_of(j * PAGE, PAGE), PAGE), :] = page
-        return after[jnp.minimum(s + 1, 64)]
-
-    lax.fori_loop(0, 32, one, after[0])
+def place(attn, pages, draft, order, attn_out, arrived, draft_out, held, sem):
+    for j in range(32):
+        pltpu.make_async_copy(pages.at[order[0, j]], held.at[j], sem.at[j // 16]).start()
     attn_out[...] = attn[...]
     draft_out[...] = draft[...]
+    outs = []
+    for half in range(2):
+        part = pl.ds(half * 16, 16)
+        pltpu.make_async_copy(held.at[part], held.at[part], sem.at[half]).wait()
+        out = pltpu.make_async_copy(held.at[part], arrived.at[part], sem.at[2 + half])
+        out.start()
+        outs.append(out)
+    for out in outs:
+        out.wait()
 
 
 def body(
@@ -462,14 +493,10 @@
         *[pltpu.VMEM((5, NODES, 128), F32)] * 4,
         pltpu.VMEM((4, 5, NODES, 128), F32),
         *[pltpu.VMEM((5, NODES, 128), F32)] * 4,
-        *[pltpu.VMEM((256, 128), BF16)] * 3,
-        *[pltpu.VMEM((8, 128), F32)] * 3,
-        pltpu.VMEM((3, 256, 128), BF16),
-        pltpu.VMEM((3, 8, 128), F32),
-        pltpu.VMEM((ZS, 32, 128), BF16),
-        pltpu.VMEM((ZS, 8, 128), F32),
-        pltpu.VMEM((ZS - 1, 32, 128), BF16),
-        pltpu.VMEM((ZS - 1, 8, 128), F32),
+        *[pltpu.VMEM((272, 128), BF16)] * 3,
+        pltpu.VMEM((3, 272, 128), BF16),
+        pltpu.VMEM((ZS, 48, 128), BF16),
+        pltpu.VMEM((ZS - 1, 48, 128), BF16),
         pltpu.VMEM((4, 8, 128), F32),
         pltpu.VMEM((4, 8, 128), F32),
         pltpu.VMEM((2, XS, 8, 8, 256), F32),
@@ -490,20 +517,27 @@
         pltpu.VMEM((XS, ZS, PAGE, 256), BF16),
         pltpu.VMEM((XS, ZS, PAGE, 256), BF16),
         pltpu.VMEM((XS, ZS, PAGE, 256), BF16),
-        *[pltpu.VMEM((ZS, PAGE, 256), BF16)] * 6,
+        *[pltpu.VMEM((2, ZS, PAGE, 256), BF16)] * 3,
+        pltpu.VMEM((64, PAGE, 256), BF16),
+        pltpu.VMEM((256, 1024), BF16),
+        pltpu.VMEM((256, 256), BF16),
+        *[pltpu.VMEM((64, 1792), BF16)] * 3,
+        pltpu.VMEM((PAGE, 256), BF16),
         pltpu.SemaphoreType.DMA((COPIES,)),
         pltpu.SemaphoreType.DMA((COPIES,)),
-        pltpu.SemaphoreType.DMA((8,)),
+        pltpu.SemaphoreType.DMA((9,)),
+        pltpu.SemaphoreType.DMA((6,)),
     ]
-    attn, pages, draft = pl.pallas_call(
+    attn, pages, draft, order = pl.pallas_call(
         kernel,
         out_shape=(
             jax.ShapeDtypeStruct((4, 1024), BF16),
-            jax.ShapeDtypeStruct((ZS, 8, PAGE, 256), BF16),
+            jax.ShapeDtypeStruct((ZS + 1, 8, PAGE, 256), BF16),
             jax.ShapeDtypeStruct((32, 64), BF16),
+            jax.ShapeDtypeStruct((8, 128), jnp.int32),
         ),
-        in_specs=[vmem, smem, vmem, vmem, vmem, smem, vmem, smem, vmem, vmem, vmem],
-        out_specs=(vmem, hbm, vmem),
+        in_specs=[hbm, smem, hbm, hbm, vmem, smem, vmem, smem, hbm, hbm, hbm, vmem],
+        out_specs=(vmem, hbm, vmem, vmem),
         scratch_shapes=scratch,
         compiler_params=pltpu.CompilerParams(
             collective_id=0, has_side_effects=True, vmem_limit_bytes=56 * 1024 * 1024
@@ -514,19 +548,24 @@
     )(
         kv_cache.reshape(64, PAGE, 256), page_session, queries, tree_kv, tree_parent, move_count,
         draft_states.T, accept_node, w_gate, w_up, w_down.T,
+        move_count,
     )
-    return pl.pallas_call(
+    attn, arrived, draft = pl.pallas_call(
         place,
         out_shape=(
             jax.ShapeDtypeStruct((4, 1024), BF16),
-            jax.ShapeDtypeStruct((32 * PAGE, 256), BF16),
+            jax.ShapeDtypeStruct((32, PAGE, 256), BF16),
             jax.ShapeDtypeStruct((32, 64), BF16),
         ),
-        in_specs=[vmem, vmem, vmem, smem],
-        out_specs=(vmem, vmem, vmem),
-        scratch_shapes=[pltpu.SMEM((65,), jnp.int32)],
-        compiler_params=pltpu.CompilerParams(vmem_limit_bytes=16 * 1024 * 1024),
-    )(attn, pages, draft, move_count)
+        in_specs=[vmem, hbm, vmem, smem],
+        out_specs=(vmem, hbm, vmem),
+        scratch_shapes=[
+            pltpu.VMEM((32, PAGE, 256), BF16),
+            pltpu.SemaphoreType.DMA((4,)),
+        ],
+        compiler_params=pltpu.CompilerParams(vmem_limit_bytes=56 * 1024 * 1024),
+    )(attn, pages.reshape(ZS * 8 + 8, PAGE, 256), draft, order)
+    return attn, arrived.reshape(32 * PAGE, 256), draft
 
 
 def solution(mesh):

time: 86.9 us -> 78.4 us (0.902)
  Pallas kernels: 83 us -> 77.4 us
  local copies, waits for them, and re-layouts: 2.98 us -> 0 us
    pallas_call x1, Pallas kernels: 79.4 us -> 73.8 us  [body(): pl.pallas_call(kernel, out_shape=(jax.ShapeDtypeStruct((4, 1024), BF16),...]
    unnamed x8 -> x0, local copies, waits for them, and re-layouts: 2.98 us -> none
where the time goes in v2:
time: 78.4 us; the launch traced here: 78 us
  Pallas kernels  77.4 us (99%)
    pallas_call x1, Pallas kernels, body(): pl.pallas_call(kernel, out_shape=(jax.ShapeDtypeStruct((4, 1024), BF16),...  73.8 us
    pallas_call x1, Pallas kernels, body(): pl.pallas_call(place, out_shape=(jax.ShapeDtypeStruct((4, 1024), BF16), j...  3.6 us

profile of v2, /device:TPU:1, one launch (start us, length us, event | category | flops | bytes accessed | tf_op | source)
XLA Modules:
  0.0 78.0 jit_solution(638353580756420443)
XLA Ops:
  0.6 73.8 %shard_map.130 = (bf16[4,1024]{1,0:T(4,128)(2,1)}, bf16[9,8,64,256]{3,2,1,0:T(8,128)(2,1)}, bf16[32,64]{1,0:T(8,128)(2,1)}, s32[8,128]{1,0:T(8,128)}) custom-call(bf16[64,64,256]{2,1,0:T(8,128)(2,1)} %bitcast.6, s32[64]{0:T(128)} %ps.1, bf16[256,1024]{1,0:T(8,128)(2,1)} %q_h.1, bf16[256,256]{1,0:T(8,128)(2,1)} %tkv_h.1, s32[4,64]{1,0:T(4,128)} %parent.1, ...), custom_call_target="tpu_custom_call" | custom-call | flops 4294967296 | bytes 5242880 | tf_op jit(solution)/shard_map/pallas_call | solution.py:531
  74.4 3.6 %shard_map.131 = (bf16[4,1024]{1,0:T(4,128)(2,1)}, bf16[32,64,256]{2,1,0:T(8,128)(2,1)}, bf16[32,64]{1,0:T(8,128)(2,1)}) custom-call(bf16[4,1024]{1,0:T(4,128)(2,1)} %get-tuple-element.10.attn, bf16[72,64,256]{2,1,0:T(8,128)(2,1)} %bitcast.5, bf16[32,64]{1,0:T(8,128)(2,1)} %get-tuple-element.12.draft, s32[8,128]{1,0:T(8,128)} %get-tuple-element.13.order), custom_call_target="tpu_custom_call" | custom-call | tf_op jit(solution)/shard_map/pallas_call | solution.py:553

commit v3 on v2

--- a/solution.py
+++ b/solution.py
@@ -343,7 +343,6 @@
     a2 = attend(2, 2)
 
     join(2, 2, a2)
-    forward(2, 0)
     arrive(g_zs)
     for j in range(7):
         slot = lax.rem(z - j + ZS, ZS)
@@ -353,7 +352,7 @@
     a3 = attend(3, 0)
 
     join(3, 0, a3)
-    forward(2, 1)
+    forward(2, 0)
 
     shard = lax.broadcasted_iota(jnp.int32, (64, 64), 0)
     other = lax.broadcasted_iota(jnp.int32, (64, 64), 1)
@@ -398,6 +397,7 @@
         info = jnp.where(spot8 == 4 + i, tree_total[at], info)
     tree_part = ([tree_sum[i * 8 : i * 8 + 8] for i in range(4)], info)
 
+    forward(2, 1)
     arrive(g_xs)
     for px in range(XS):
         slot = lax.rem(x - px + XS, XS)

time: 78.4 us -> 82 us (1.046)
  the two profiles are of different devices: /device:TPU:1 before, /device:TPU:5 now
where the time goes in v3:
time: 82 us; the launch traced here: 81.6 us
  Pallas kernels  80.9 us (99%)
    pallas_call x1, Pallas kernels, body(): pl.pallas_call(kernel, out_shape=(jax.ShapeDtypeStruct((4, 1024), BF16),...  77.3 us
    pallas_call x1, Pallas kernels, body(): pl.pallas_call(place, out_shape=(jax.ShapeDtypeStruct((4, 1024), BF16), j...  3.67 us

profile of v3, /device:TPU:5, one launch (start us, length us, event | category | flops | bytes accessed | tf_op | source)
XLA Modules:
  0.0 81.6 jit_solution(5519217559146403057)
XLA Ops:
  0.6 77.3 %shard_map.130 = (bf16[4,1024]{1,0:T(4,128)(2,1)}, bf16[9,8,64,256]{3,2,1,0:T(8,128)(2,1)}, bf16[32,64]{1,0:T(8,128)(2,1)}, s32[8,128]{1,0:T(8,128)}) custom-call(bf16[64,64,256]{2,1,0:T(8,128)(2,1)} %bitcast.6, s32[64]{0:T(128)} %ps.1, bf16[256,1024]{1,0:T(8,128)(2,1)} %q_h.1, bf16[256,256]{1,0:T(8,128)(2,1)} %tkv_h.1, s32[4,64]{1,0:T(4,128)} %parent.1, ...), custom_call_target="tpu_custom_call" | custom-call | flops 4294967296 | bytes 5242880 | tf_op jit(solution)/shard_map/pallas_call | solution.py:531
  77.9 3.7 %shard_map.131 = (bf16[4,1024]{1,0:T(4,128)(2,1)}, bf16[32,64,256]{2,1,0:T(8,128)(2,1)}, bf16[32,64]{1,0:T(8,128)(2,1)}) custom-call(bf16[4,1024]{1,0:T(4,128)(2,1)} %get-tuple-element.10.attn, bf16[72,64,256]{2,1,0:T(8,128)(2,1)} %bitcast.5, bf16[32,64]{1,0:T(8,128)(2,1)} %get-tuple-element.12.draft, s32[8,128]{1,0:T(8,128)} %get-tuple-element.13.order), custom_call_target="tpu_custom_call" | custom-call | tf_op jit(solution)/shard_map/pallas_call | solution.py:553
